TPU v7x, 128 devices: a whole 4x4x4 slice. The times are simulated.
128 devices in a mesh: dp: 16 (over y_hi, x, core), mp: 8 (over z, y_lo).
Axes of the slice: x: 4, y: 4 (y_hi: 2, y_lo: 2; y = y_hi * 2 + y_lo), z: 4, core: 2. Of those that a mesh axis runs over, the one named last changes fastest.
Arguments:
- acts: bfloat16 [2048, 4608], P('dp', 'mp'), may hold values from -6 to 6
- old_weights: bfloat16 [2, 4608, 18432], P(None, ('mp', 'dp')), may hold values from -4 to 4
- old_mean: bfloat16 [2, 4608, 18432], P(None, ('mp', 'dp')), may hold values from -2 to 2
- old_var: float32 [2, 4608, 18432], P(None, ('mp', 'dp')), may hold values from 0.05 to 0.5
- cotangent: bfloat16 [2048, 18432], P('mp', 'dp'), may hold values from -6 to 6
Outputs:
- hidden: bfloat16 [2048, 18432], P('mp', 'dp')
- input_grad: bfloat16 [2048, 4608], P('dp', 'mp')
- new_weights: bfloat16 [2, 4608, 18432], P(None, 'mp', 'dp')
- new_mean: bfloat16 [2, 4608, 18432], P(None, 'mp', 'dp')
- new_var: float32 [2, 4608, 18432], P(None, 'mp', 'dp')
All inputs are finite; a program needn't handle non-finite values.
Results may differ from a plain program's by a relative error of at most 0.005.
Values may be sent and summed in bfloat16 or wider, within the bound.
A program may use at most 192 MiB of HBM per device.

v0:
```python
import jax
import jax.numpy as jnp
from jax import lax
from jax.sharding import PartitionSpec as P

D = 4608
RESUME_STEP = 1000


tanh_coef = 0.7978845608028654
cube_coef = 0.044715
beta_one = 0.9
beta_two = 0.95
learn_rate = 0.05
decay_rate = 0.1
epsilon = 1e-08


def gelu_value(value):
    return 0.5 * value * (1.0 + jnp.tanh(tanh_coef * (value + cube_coef * value * value * value)))


def gelu_slope(value):
    inner = jnp.tanh(tanh_coef * (value + cube_coef * value * value * value))
    return 0.5 * (1.0 + inner) + 0.5 * value * (1.0 - inner * inner) * tanh_coef * (
        1.0 + 3.0 * cube_coef * value * value
    )


def adam_update(weights, mean, variance, weight_grads):
    moment_one = beta_one * mean.astype(jnp.float32) + (1.0 - beta_one) * weight_grads
    var_next = beta_two * variance + (1.0 - beta_two) * weight_grads * weight_grads
    mean_hat = moment_one / (1.0 - beta_one**RESUME_STEP)
    var_hat = var_next / (1.0 - beta_two**RESUME_STEP)
    master = weights.astype(jnp.float32)
    updated = master - learn_rate * (mean_hat / (jnp.sqrt(var_hat) + epsilon) + decay_rate * master)
    return (updated.astype(jnp.bfloat16), moment_one.astype(jnp.bfloat16), var_next)


def relay_variance(old_var):
    return lax.all_to_all(old_var, "dp", split_axis=2, concat_axis=1, tiled=True)


def shards(acts, old_weights, old_mean, old_var, cotangent):
    width_scale = D ** (-0.5)
    weights, first_moment = (
        lax.all_to_all(old_weights, "dp", split_axis=2, concat_axis=1, tiled=True),
        lax.all_to_all(old_mean, "dp", split_axis=2, concat_axis=1, tiled=True),
    )
    variance = relay_variance(old_var)
    token_cols = lax.all_gather(acts, "dp", axis=0, tiled=True)
    projected = lax.psum_scatter(
        jnp.einsum("td,kdf->tkf", token_cols, weights, preferred_element_type=jnp.float32),
        "mp",
        scatter_dimension=0,
        tiled=True,
    )
    gate = projected[:, 0, :] * width_scale
    up_proj = projected[:, 1, :] * width_scale
    activated = gelu_value(gate)
    hidden = (activated * up_proj).astype(jnp.bfloat16)
    upstream = cotangent.astype(jnp.float32)
    gate_grad = (upstream * up_proj * gelu_slope(gate)).astype(jnp.bfloat16)
    up_grad = (upstream * activated).astype(jnp.bfloat16)
    local_grads = jnp.stack([gate_grad, up_grad], axis=1)
    all_grads = lax.all_gather(local_grads, "mp", axis=0, tiled=True)
    weight_grads = (
        jnp.einsum("td,tkf->kdf", token_cols, all_grads, preferred_element_type=jnp.float32)
        * width_scale
    )
    input_terms = lax.psum_scatter(
        jnp.einsum("tkf,kdf->td", all_grads, weights, preferred_element_type=jnp.float32)
        * width_scale,
        "dp",
        scatter_dimension=0,
        tiled=True,
    )
    input_grad = input_terms.astype(jnp.bfloat16)
    new_weights, new_mean, new_var = adam_update(weights, first_moment, variance, weight_grads)
    return (hidden, input_grad, new_weights, new_mean, new_var)


def solution(mesh):
    placed = (
        P("dp", "mp"),
        P(None, ("mp", "dp"), None),
        P(None, ("mp", "dp"), None),
        P(None, ("mp", "dp"), None),
        P("mp", "dp"),
    )
    return jax.shard_map(
        shards,
        mesh=mesh,
        in_specs=placed,
        out_specs=(
            P("mp", "dp"),
            P("dp", "mp"),
            P(None, "mp", "dp"),
            P(None, "mp", "dp"),
            P(None, "mp", "dp"),
        ),
        check_vma=False,
    )
```

profile of v0, /device:TPU:1, one launch (start us, length us, event | category | flops | bytes accessed | tf_op | source)
XLA Modules:
  0.0 1037.3 jit_solution(1147938605280088250)
XLA Ops:
  7.2 0.0 all-gather.3.cloned.1.call-start
  7.2 0.7 all-gather.3.cloned.1.call-update
  7.9 0.0 reduce-scatter.3.cloned.1.call-start
  7.9 22.9 %copy.32 = bf16[2,36,18432]{1,0,2:T(2,128)(2,1)} copy(bf16[2,36,18432]{2,0,1:T(2,128)(2,1)} %param.6) | data formatting | bytes 5308416 | tf_op args[1]
  30.9 18.3 %reshape.32 = bf16[16,2,41472]{2,1,0:T(2,128)(2,1)S(1)} reshape(bf16[18432,2,36]{2,1,0:T(2,128)(2,1)} %bitcast.114) | data formatting | bytes 5308416
  49.1 43.4 %all_to_all.36 = bf16[16,2,41472]{2,1,0:T(2,128)(2,1)} all-to-all(bf16[16,2,41472]{2,1,0:T(2,128)(2,1)S(1)} %reshape.32), channel_id=1, replica_groups=mesh['dp'=16,'mp'=8] {'dp'}, dimensions={0} | all-to-all | bytes 5308416 | tf_op jit(solution)/shard_map/all_to_all | solution.py:47
  92.5 27.3 %reshape.33 = bf16[18432,2,36]{2,1,0:T(2,128)(2,1)} reshape(bf16[16,2,41472]{2,1,0:T(2,128)(2,1)} %all_to_all.36) | data formatting | bytes 5308416
  119.8 21.9 %copy.33 = bf16[2,36,16,1152]{3,0,1,2:T(2,128)(2,1)S(1)} copy(bf16[2,36,16,1152]{1,0,3,2:T(2,128)(2,1)} %bitcast.113) | data formatting | bytes 5308416 | tf_op jit(solution)/shard_map/all_to_all | solution.py:47
  141.7 0.0 copy-start.1
  141.7 0.0 all-gather.3.cloned.1.call-done
  141.8 13.4 %fusion.5 = f32[2048,2,1152]{2,0,1:T(8,128)} fusion(bf16[2048,576]{0,1:T(8,128)(2,1)} %all-gather.3.cloned.1.call-done, bf16[2,576,1152]{2,0,1:T(2,128)(2,1)S(1)} %bitcast.118), kind=kOutput, calls=%fused_computation.12 | convolution fusion | flops 5435817984 | bytes 23887872 | tf_op jit(solution)/shard_map/td,kdf->tkf/dot_general | solution.py:53
  155.2 0.0 copy-done.1
  155.2 0.0 copy-start.3
  155.2 0.0 reduce-scatter.3.cloned.1.call-update
  155.2 0.0 all-gather.5.cloned.1.call-start
  155.2 364.4 %reduce-scatter.3.cloned.1.call-done = f32[256,2,1152]{2,0,1:T(8,128)} async-done(((f32[2048,2,1152]{2,0,1:T(8,128)}), f32[256,2,1152]{2,0,1:T(8,128)}) %reduce-scatter.3.cloned.1.call-update) | async-done | bytes 2359312 | tf_op jit(solution)/shard_map/reduce_scatter | solution.py:52
  519.7 0.0 copy-done.3
  519.7 3.6 fusion.22
  523.2 0.0 copy-start
  523.2 1.2 pad_maximum_fusion
  524.4 0.0 all-gather.5.cloned.1.call-update
  524.4 1.0 copy-done
  525.4 16.9 %copy.37 = bf16[2,36,18432]{1,0,2:T(2,128)(2,1)} copy(bf16[2,36,18432]{2,0,1:T(2,128)(2,1)S(1)} %copy-done) | data formatting | bytes 5308416 | tf_op args[2]
  542.3 19.3 %reshape.36 = bf16[16,2,41472]{2,1,0:T(2,128)(2,1)} reshape(bf16[18432,2,36]{2,1,0:T(2,128)(2,1)} %bitcast.115) | data formatting | bytes 5308416
  561.7 7.0 all-to-all-start.1
  568.7 25.2 %copy.40 = f32[2,36,18432]{1,0,2:T(2,128)} copy(f32[2,36,18432]{2,0,1:T(2,128)} %param.8) | data formatting | bytes 10616832 | tf_op args[3]
  593.9 36.8 %reshape.34 = f32[16,1,82944]{2,1,0:T(1,128)} reshape(f32[18432,2,36]{2,1,0:T(2,128)} %bitcast.112) | data formatting | bytes 10616832
  630.7 0.0 all-to-all-done.1
  630.7 7.2 all-to-all-start.2
  637.9 0.2 reduce-scatter.5.cloned.1.call-start
  638.2 160.7 %all-gather.5.cloned.1.call-done = bf16[2048,2,1152]{2,0,1:T(8,128)(2,1)} async-done(((bf16[256,2,1152]{2,0,1:T(8,128)(2,1)}), bf16[2048,2,1152]{2,0,1:T(8,128)(2,1)}) %all-gather.5.cloned.1.call-update) | async-done | bytes 9437200 | tf_op jit(solution)/shard_map/all_gather | solution.py:66
  798.9 11.6 %bitcast_multiply_fusion = f32[2048,576]{0,1:T(8,128)} fusion(bf16[2048,2,1152]{2,0,1:T(8,128)(2,1)} %all-gather.5.cloned.1.call-done, bf16[2,576,1152]{2,0,1:T(2,128)(2,1)} %bitcast.119), kind=kOutput, calls=%fused_computation.9 | convolution fusion | flops 5436997632 | bytes 16809984 | tf_op jit(solution)/shard_map/tkf,kdf->td/dot_general | solution.py:72
  810.5 0.0 reduce-scatter.5.cloned.1.call-update
  810.5 27.4 %reshape.37 = bf16[18432,2,36]{2,1,0:T(2,128)(2,1)} reshape(bf16[16,2,41472]{2,1,0:T(2,128)(2,1)S(1)} %all-to-all-done.1) | data formatting | bytes 5308416
  837.9 12.2 %convert_multiply_fusion = f32[2,36,18432]{1,0,2:T(2,128)} fusion(bf16[18432,2,36]{2,1,0:T(2,128)(2,1)} %reshape.37), kind=kLoop, calls=%fused_computation | loop fusion | flops 2654208 | bytes 7962624 | tf_op jit(solution)/shard_map/mul | solution.py:31
  850.1 25.4 %copy.38 = f32[2,36,16,1152]{3,0,1,2:T(2,128)} copy(f32[2,36,16,1152]{1,0,3,2:T(2,128)} %bitcast.110) | data formatting | bytes 10616832 | tf_op jit(solution)/shard_map/mul | solution.py:31
  875.5 0.0 all-to-all-done.2
  875.5 0.5 broadcast.88
  876.1 52.2 %reduce = f32[16,82944]{1,0:T(8,128)} reduce(f32[16,1,82944]{2,1,0:T(1,128)} %all-to-all-done.2, f32[]{:T(128)} %broadcast.88), dimensions={1}, to_apply=%all_to_all.32.reduce_sub_computation | reduce | bytes 10616836 | tf_op jit(solution)/shard_map/all_to_all | solution.py:41
  928.3 43.7 %reshape.35 = f32[18432,2,36]{2,1,0:T(2,128)} reshape(f32[16,82944]{1,0:T(8,128)} %reduce) | data formatting | bytes 10616832
  972.0 13.5 %broadcast_multiply_fusion = f32[2,36,18432]{1,0,2:T(2,128)} fusion(f32[18432,2,36]{2,1,0:T(2,128)} %reshape.35), kind=kLoop, calls=%fused_computation.1 | loop fusion | flops 1327104 | bytes 10616832 | tf_op jit(solution)/shard_map/mul | solution.py:32
  985.4 0.0 copy-start.2
  985.4 25.6 %copy.41 = f32[2,36,16,1152]{3,0,1,2:T(2,128)} copy(f32[2,36,16,1152]{1,0,3,2:T(2,128)} %bitcast.111) | data formatting | bytes 10616832 | tf_op jit(solution)/shard_map/mul | solution.py:32
  1011.0 0.0 copy-done.2
  1011.0 18.2 %fusion.2 = (bf16[2,576,1152]{2,1,0:T(8,128)(2,1)}, f32[2,576,1152]{2,1,0:T(8,128)}, bf16[2,576,1152]{2,1,0:T(8,128)(2,1)}) fusion(bf16[2,576,1152]{2,0,1:T(2,128)(2,1)S(1)} %bitcast.120, f32[2,576,1152]{2,0,1:T(2,128)} %bitcast.116, f32[2,576,1152]{2,0,1:T(2,128)} %bitcast.117, bf16[2048,2,1152]{2,0,1:T(8,128)(2,1)} %all-gather.5.cloned.1.call-done, ...), kind=kOutput, calls=%fused_computation.6 | convolution fusion | flops 5455724544 | bytes 35684352 | tf_op jit(solution)/shard_map/td,tkf->kdf/dot_general | solution.py:68
  1029.2 0.0 reduce-scatter.5.cloned.1.call-done
  1029.2 1.6 convert_element_type.34
Async XLA Ops:
  7.2 134.6 %all-gather.3.cloned.1.call-start = ((), (), s32[]{:S(2)}) async-start(), calls=%async_computation.5 | async-start | bytes 2506752 | tf_op jit(solution)/shard_map/all_gather | solution.py:51
  7.9 511.8 %reduce-scatter.3.cloned.1.call-start = ((), (), s32[]{:S(2)}) async-start(), calls=%async_computation.6 | async-start | bytes 21233664 | tf_op jit(solution)/shard_map/reduce_scatter | solution.py:52
  141.7 13.4 %copy-start.1 = (bf16[2,36,16,1152]{3,0,1,2:T(2,128)(2,1)}, bf16[2,36,16,1152]{3,0,1,2:T(2,128)(2,1)S(1)}, u32[]{:S(2)}) copy-start(bf16[2,36,16,1152]{3,0,1,2:T(2,128)(2,1)S(1)} %copy.33) | copy-start | bytes 7962628
  155.2 364.5 %copy-start.3 = (bf16[256,1152]{1,0:T(8,128)(2,1)S(1)}, bf16[256,1152]{1,0:T(8,128)(2,1)}, u32[]{:S(2)}) copy-start(bf16[256,1152]{1,0:T(8,128)(2,1)} %param.9) | copy-start | bytes 1769476
  155.2 643.7 %all-gather.5.cloned.1.call-start = ((), (), s32[]{:S(2)}) async-start(), calls=%async_computation.7 | async-start | bytes 10616832 | tf_op jit(solution)/shard_map/all_gather | solution.py:66
  523.2 2.2 copy-start
  561.7 69.0 %all-to-all-start.1 = ((bf16[16,2,41472]{2,1,0:T(2,128)(2,1)}), bf16[16,2,41472]{2,1,0:T(2,128)(2,1)S(1)}, u32[]{:S(2)}, u32[]{:S(2)}) async-start(bf16[16,2,41472]{2,1,0:T(2,128)(2,1)} %reshape.36), calls=%async_computation.3 | async-start | bytes 5308416 | tf_op jit(solution)/shard_map/all_to_all | solution.py:48
  630.7 244.8 %all-to-all-start.2 = ((f32[16,1,82944]{2,1,0:T(1,128)}), f32[16,1,82944]{2,1,0:T(1,128)}, u32[]{:S(2)}, u32[]{:S(2)}) async-start(f32[16,1,82944]{2,1,0:T(1,128)} %reshape.34), calls=%async_computation.4 | async-start | bytes 10616832 | tf_op jit(solution)/shard_map/all_to_all | solution.py:41
  637.9 391.2 %reduce-scatter.5.cloned.1.call-start = ((), (), s32[]{:S(2)}) async-start(), calls=%async_computation.8 | async-start | bytes 5013504 | tf_op jit(solution)/shard_map/reduce_scatter | solution.py:71
  985.4 25.6 %copy-start.2 = (bf16[2,36,16,1152]{3,0,1,2:T(2,128)(2,1)S(1)}, bf16[2,36,16,1152]{3,0,1,2:T(2,128)(2,1)}, u32[]{:S(2)}) copy-start(bf16[2,36,16,1152]{3,0,1,2:T(2,128)(2,1)} %copy-done.1) | copy-start | bytes 7962628
Sparse Core Ops, SparseCore 0:
  10.3 57.7 all-gather.2
  155.3 364.3 reduce-scatter.2
  524.6 274.2 all-gather.4
  810.6 82.6 reduce-scatter.4
where the time goes:
time: 1040 us
  waiting for transfers between devices  526 us (51%)
  local copies, waits for them, and re-layouts  312 us (30%)
  other arithmetic  84.2 us (8%)
  blocking collectives  43.4 us (4%)
  matrix products  43.1 us (4%)
  starting transfers between devices  14.6 us (1%)
  between operations  13.8 us (1%)
    reduce_scatter x1, waiting for transfers between devices, shards(): lax.psum_scatter(jnp.einsum('td,kdf->tkf', token_cols, weights, preferred...  364 us
    unnamed x17, local copies, waits for them, and re-layouts  239 us
    all_gather x1, waiting for transfers between devices, shards(): all_grads = lax.all_gather(local_grads, 'mp', axis=0, tiled=True)  161 us
    all_to_all x1, other arithmetic, relay_variance(): lax.all_to_all(old_var, 'dp', split_axis=2, concat_axis=1, tiled=True)  52.2 us
    all_to_all x1, blocking collectives, shards(): lax.all_to_all(old_weights, 'dp', split_axis=2, concat_axis=1, tiled=True)  43.4 us
    mul x1, local copies, waits for them, and re-layouts, adam_update(): beta_two * variance + (1.0 - beta_two) * weight_grads * weight_grads  25.6 us
    mul x1, local copies, waits for them, and re-layouts, adam_update(): beta_one * mean.astype(jnp.float32) + (1.0 - beta_one) * weight_grads  25.4 us
    all_to_all x1, local copies, waits for them, and re-layouts, shards(): lax.all_to_all(old_weights, 'dp', split_axis=2, concat_axis=1, tiled=True)  21.9 us
  transfers between devices with their start and end apart: 6, of which 2 were waited for; matrix products, arithmetic and copies ran while one was open for 40% of the time, Pallas kernels for 0%

commit v1 on v0

v1 whole, which is shorter than its diff:
```python
import functools

import jax
import jax.numpy as jnp
from jax import lax
from jax.experimental import pallas as pl
from jax.experimental.pallas import tpu as pltpu
from jax.sharding import PartitionSpec as P

D = 4608
RESUME_STEP = 1000

tanh_coef = 0.7978845608028654
cube_coef = 0.044715
beta_one = 0.9
beta_two = 0.95
learn_rate = 0.05
decay_rate = 0.1
epsilon = 1e-08
width_scale = D ** (-0.5)

MESH = pl.DeviceIdType.MESH
F32 = jnp.float32
BF16 = jnp.bfloat16

DP, Z, LO = 16, 4, 2
ROWS = 36
WIDTH = ROWS * DP
TOK = 2048
BLOCK = TOK // Z
HALF = BLOCK // LO
FS = 1152
CH = 3
FC = FS // CH
OWN = TOK // DP


def gelu_parts(value):
    inner = jnp.tanh(tanh_coef * (value + cube_coef * value * value * value))
    activated = 0.5 * value * (1.0 + inner)
    slope = 0.5 * (1.0 + inner) + 0.5 * value * (1.0 - inner * inner) * tanh_coef * (
        1.0 + 3.0 * cube_coef * value * value
    )
    return activated, slope


def dot(left, right):
    return jnp.dot(left, right, preferred_element_type=F32)


def kernel(
    at_in, w_in, m_in, v_in, cot, hid, ig, nw, nm, nv,
    at, a, wr, mr, vr, wd, sb, rmid, rfin, yls, ylr, grads, acc, gw, nws, nms, nvs, xs, xr, xf,
    copy_sem, out_sem, act_send, act_recv, fwd_send, fwd_recv, rel_send, rel_recv,
    zs_sem, zr_sem, x_send, x_recv,
):
    dp, mp = lax.axis_index("dp"), lax.axis_index("mp")
    core = lax.rem(dp, 2)
    line = lax.div(dp, 2)
    x = lax.rem(line, 4)
    y_hi = lax.div(line, 4)
    z = lax.div(mp, 2)
    lo = lax.rem(mp, 2)

    def z_dev(step):
        return (dp, lax.rem(z + step, Z) * 2 + lo)

    plus, minus = z_dev(1), z_dev(Z - 1)
    mate = (dp, z * 2 + 1 - lo)
    twin = (dp + 1 - 2 * core, mp)

    def peer_dp(i):
        far = 1 - lax.rem(i, 2)
        j = lax.div(i, 2) + lax.rem(i, 2)
        q = lax.div(j, 2)
        step = q + lax.div(q, 2) * (1 - 2 * lax.rem(q, 2))
        other = lax.rem(core + lax.rem(j, 2), 2)
        return lax.rem(y_hi + far, 2) * 8 + lax.rem(x + step, 4) * 2 + other

    def peer_line(i):
        far = lax.rem(i, 2)
        q = lax.div(i, 2)
        step = q + lax.div(q, 2) * (1 - 2 * lax.rem(q, 2))
        return lax.rem(y_hi + far, 2) * 4 + lax.rem(x + step, 4)

    barrier = pltpu.get_barrier_semaphore()

    @pl.loop(0, DP - 1)
    def _(i):
        pl.semaphore_signal(barrier, inc=1, device_id=(peer_dp(i), mp), device_id_type=MESH)

    for other in (plus, minus, mate):
        pl.semaphore_signal(barrier, inc=1, device_id=other, device_id_type=MESH)
    pl.semaphore_wait(barrier, DP - 1 + 3)

    def remote(src, dst, send, recv, device):
        return pltpu.make_async_remote_copy(
            src_ref=src, dst_ref=dst, send_sem=send, recv_sem=recv, device_id=device, device_id_type=MESH
        )

    def cols(index):
        return pl.ds(pl.multiple_of(index * OWN, OWN), OWN)

    own_act = pltpu.make_async_copy(at_in, at.at[:, cols(dp)], copy_sem)
    own_act.start()

    @pl.loop(1, 8)
    def _(i):
        remote(at_in, at.at[:, cols(dp)], act_send, act_recv.at[i - 1], (peer_line(i) * 2 + core, mp)).start()

    remote(at_in, at.at[:, cols(dp)], fwd_send, fwd_recv, twin).start()

    def relay(index, src, dst, c):
        mine = pl.ds(dp * ROWS, ROWS)

        def part(owner):
            return src.at[:, :, pl.ds(pl.multiple_of(owner * FS + c * FC, 128), FC)]

        pltpu.make_async_copy(part(dp), dst.at[c, mine], rel_recv.at[index, c]).start()

        @pl.loop(0, DP - 1)
        def _(i):
            owner = peer_dp(i)
            remote(part(owner), dst.at[c, mine], rel_send.at[index, c], rel_recv.at[index, c], (owner, mp)).start()

    def relayed(index, dst, c):
        pltpu.make_async_copy(dst.at[c], dst.at[c], rel_recv.at[index, c]).wait()

    def relay_sent(index, dst, c):
        sent = dst.at[c, pl.ds(0, WIDTH - ROWS)]
        pltpu.make_async_copy(sent, sent, rel_send.at[index, c]).wait()

    for c in range(CH):
        relay(0, w_in, wr, c)

    own_act.wait()

    @pl.loop(1, 8)
    def _(i):
        far = lax.rem(i, 2)
        q = lax.div(i, 2)
        step = q + lax.div(q, 2) * (1 - 2 * lax.rem(q, 2))
        source = (lax.rem(y_hi + far, 2) * 4 + lax.rem(x + 4 - step, 4)) * 2 + core
        block = at.at[:, cols(source)]
        remote(block, block, act_send, act_recv.at[i - 1], twin).wait_recv()
        remote(block, block, fwd_send, fwd_recv, twin).start()

    half_acts = at.at[:, pl.ds(0, TOK // 2)]
    pltpu.make_async_copy(half_acts, half_acts, fwd_recv).wait()

    @pl.loop(0, DP)
    def _(i):
        a[pl.ds(pl.multiple_of(i * OWN, OWN), OWN), :] = at[:, cols(i)].T

    def tokens(step, half):
        return pl.ds(pl.multiple_of(lax.rem(z + step, Z) * BLOCK + half * HALF, HALF), HALF)

    sends = []

    def zsend(c, slot, src, dst, device):
        copy = remote(src, dst, zs_sem.at[c, slot], zr_sem.at[c, slot], device)
        copy.start()
        sends.append(copy)

    def zwait(c, slot, dst):
        remote(dst, dst, zs_sem.at[c, slot], zr_sem.at[c, slot], plus).wait_recv()

    def first(c):
        relayed(0, wr, c)

        @pl.loop(0, WIDTH // 32)
        def _(i):
            rows = pl.ds(pl.multiple_of(i * 32, 32), 32)
            pair = jnp.swapaxes(wr[c, rows], 0, 1)
            wd[c, rows, 0:FC] = pair[0]
            wd[c, rows, FC : 2 * FC] = pair[1]

        @pl.loop(0, 4)
        def _(slot):
            late = lax.div(slot, 2)
            odd = lax.rem(slot, 2)
            step = 2 + late * (2 * odd - 1)
            half = odd + late * (1 - 2 * odd)
            sb[c, slot] = dot(a[tokens(step, half), :], wd[c]).astype(BF16)

        zsend(c, 0, sb.at[c, 0], rmid.at[c, 0], plus)
        zsend(c, 1, sb.at[c, 1], rmid.at[c, 1], minus)
        zsend(c, 2, sb.at[c, 2], rfin.at[c, 0, 1], plus)
        zsend(c, 3, sb.at[c, 3], rfin.at[c, 1, 0], minus)

    def second(c):
        zwait(c, 0, rmid.at[c, 0])
        zwait(c, 1, rmid.at[c, 1])

        @pl.loop(0, 2)
        def _(slot):
            sb[c, 4 + slot] = (
                dot(a[tokens(1 + 2 * slot, slot), :], wd[c]) + rmid[c, slot].astype(F32)
            ).astype(BF16)

        zsend(c, 4, sb.at[c, 4], rfin.at[c, 0, 0], plus)
        zsend(c, 5, sb.at[c, 5], rfin.at[c, 1, 1], minus)

    def block_sum(c, half):
        return (
            dot(a[tokens(0, half), :], wd[c])
            + rfin[c, 0, half].astype(F32)
            + rfin[c, 1, half].astype(F32)
        )

    def third(c):
        zwait(c, 2, rfin.at[c, 0, 1])
        zwait(c, 3, rfin.at[c, 1, 0])
        zwait(c, 4, rfin.at[c, 0, 0])
        zwait(c, 5, rfin.at[c, 1, 1])
        yls[c] = block_sum(c, 1 - lo).astype(BF16)
        zsend(c, 6, yls.at[c], ylr.at[c], mate)

    def fourth(c):
        zwait(c, 6, ylr.at[c])
        sums = (block_sum(c, lo) + ylr[c].astype(F32)) * width_scale
        gate, up = sums[:, :FC], sums[:, FC:]
        span = slice(c * FC, (c + 1) * FC)
        activated, slope = gelu_parts(gate)
        upstream = cot[:, span].astype(F32)
        hid[:, span] = (activated * up).astype(BF16)
        rows = tokens(0, lo)
        grads[c, rows, 0:FC] = (upstream * up * slope).astype(BF16)
        grads[c, rows, FC : 2 * FC] = (upstream * activated).astype(BF16)
        mine = grads.at[c, rows]
        zsend(c, 7, mine, mine, mate)
        zsend(c, 8, mine, mine, plus)
        zsend(c, 9, mine, mine, minus)

    def fifth(c):
        theirs = grads.at[c, tokens(0, 1 - lo)]
        zwait(c, 7, theirs)
        zsend(c, 10, theirs, theirs, plus)
        zsend(c, 11, theirs, theirs, minus)

    def sixth(c):
        below, above = grads.at[c, tokens(3, lo)], grads.at[c, tokens(1, 1 - lo)]
        zwait(c, 8, below)
        zsend(c, 12, below, below, plus)
        zwait(c, 11, above)
        zsend(c, 13, above, above, minus)

    def gathered(c):
        zwait(c, 9, grads.at[c, tokens(1, lo)])
        zwait(c, 10, grads.at[c, tokens(3, 1 - lo)])
        zwait(c, 12, grads.at[c, tokens(2, lo)])
        zwait(c, 13, grads.at[c, tokens(2, 1 - lo)])

    def back(c):
        @pl.loop(0, TOK // HALF)
        def _(i):
            rows = pl.ds(pl.multiple_of(i * HALF, HALF), HALF)
            term = lax.dot_general(
                grads[c, rows, :], wd[c], (((1,), (1,)), ((), ())), preferred_element_type=F32
            )
            if c == 0:
                acc[rows, :] = term
            else:
                acc[rows, :] += term

    outs = ((nws, nw), (nms, nm), (nvs, nv))

    def written(c):
        span = pl.ds(c * FC, FC)
        return [
            pltpu.make_async_copy(held, out.at[:, :, span], out_sem.at[i]) for i, (held, out) in enumerate(outs)
        ]

    def weight_grads(c):
        @pl.loop(0, 6)
        def _(i):
            k = lax.rem(i, 2)
            rows = pl.ds(pl.multiple_of(lax.div(i, 2) * 192, 192), 192)
            span = pl.ds(pl.multiple_of(k * FC, FC), FC)
            gw[k, rows, :] = dot(at[rows, :], grads[c, :, span]) * width_scale

    def update(c):
        relayed(1, mr, c)
        relayed(2, vr, c)
        if c > 0:
            for copy in written(c - 1):
                copy.wait()

        @pl.loop(0, WIDTH // 32)
        def _(i):
            rows = pl.ds(pl.multiple_of(i * 32, 32), 32)
            mean = jnp.swapaxes(mr[c, rows], 0, 1)
            var = jnp.swapaxes(vr[c, rows], 0, 1)
            for k in range(2):
                grad = gw[k, rows, :]
                moment_one = beta_one * mean[k].astype(F32) + (1.0 - beta_one) * grad
                var_next = beta_two * var[k].astype(F32) + (1.0 - beta_two) * grad * grad
                mean_hat = moment_one / (1.0 - beta_one**RESUME_STEP)
                var_hat = var_next / (1.0 - beta_two**RESUME_STEP)
                master = wd[c, rows, k * FC : (k + 1) * FC].astype(F32)
                updated = master - learn_rate * (
                    mean_hat / (jnp.sqrt(var_hat) + epsilon) + decay_rate * master
                )
                nws[k, rows, :] = updated.astype(BF16)
                nms[k, rows, :] = moment_one.astype(BF16)
                nvs[k, rows, :] = var_next

        for copy in written(c):
            copy.start()

    first(0)
    relay(1, m_in, mr, 0)
    first(1)
    second(0)
    relay(2, v_in, vr, 0)
    first(2)
    second(1)
    relay(1, m_in, mr, 1)
    third(0)
    fourth(0)
    second(2)
    relay(2, v_in, vr, 1)
    fifth(0)
    third(1)
    fourth(1)
    relay(1, m_in, mr, 2)
    sixth(0)
    fifth(1)
    third(2)
    fourth(2)
    relay(2, v_in, vr, 2)
    gathered(0)
    fifth(2)
    sixth(1)
    back(0)
    weight_grads(0)
    update(0)
    sixth(2)
    gathered(1)
    back(1)
    weight_grads(1)
    update(1)
    gathered(2)
    back(2)

    def acc_rows(index):
        return pl.ds(pl.multiple_of(index * OWN, OWN), OWN)

    @pl.loop(0, 8)
    def _(j):
        xs[j] = acc[acc_rows(j * 2 + 1 - core), :].astype(BF16)

    swap = remote(xs, xr, x_send.at[0], x_recv.at[0], twin)
    swap.start()
    weight_grads(2)
    swap.wait()

    @pl.loop(0, 8)
    def _(j):
        rows = acc_rows(j * 2 + core)
        total = acc[rows, :] + xr[j].astype(F32)
        acc[rows, :] = total
        xs[j] = total.astype(BF16)

    @pl.loop(1, 8)
    def _(i):
        owner = peer_line(i)
        remote(xs.at[owner], xf.at[i - 1], x_send.at[1], x_recv.at[1], (owner * 2 + core, mp)).start()

    update(2)
    pltpu.make_async_copy(xf, xf, x_recv.at[1]).wait()
    total = acc[acc_rows(dp), :]
    for i in range(7):
        total = total + xf[i].astype(F32)
    ig[...] = (total * width_scale).T.astype(BF16)

    pltpu.make_async_copy(xf, xf, x_send.at[1]).wait()
    for copy in written(CH - 1):
        copy.wait()
    for copy in sends:
        copy.wait_send()
    for c in range(CH):
        relay_sent(0, wr, c)
        relay_sent(1, mr, c)
        relay_sent(2, vr, c)
    seven = at.at[:, pl.ds(0, 7 * OWN)]
    pltpu.make_async_copy(seven, seven, act_send).wait()
    pltpu.make_async_copy(half_acts, half_acts, fwd_send).wait()


def shards(acts, old_weights, old_mean, old_var, cotangent):
    vmem = pl.BlockSpec(memory_space=pltpu.VMEM)
    hbm = pl.BlockSpec(memory_space=pl.ANY)
    dma = pltpu.SemaphoreType.DMA
    macs = 3 * TOK * WIDTH * 2 * FS

    hidden, input_grad, new_weights, new_mean, new_var = pl.pallas_call(
        kernel,
        out_shape=(
            jax.ShapeDtypeStruct((HALF, FS), BF16),
            jax.ShapeDtypeStruct((WIDTH, OWN), BF16),
            jax.ShapeDtypeStruct((2, WIDTH, FS), BF16),
            jax.ShapeDtypeStruct((2, WIDTH, FS), BF16),
            jax.ShapeDtypeStruct((2, WIDTH, FS), F32),
        ),
        in_specs=[hbm, hbm, hbm, hbm, vmem],
        out_specs=(vmem, vmem, hbm, hbm, hbm),
        scratch_shapes=[
            pltpu.VMEM((WIDTH, TOK), BF16),
            pltpu.VMEM((TOK, WIDTH), BF16),
            pltpu.VMEM((CH, WIDTH, 2, FC), BF16),
            pltpu.VMEM((CH, WIDTH, 2, FC), BF16),
            pltpu.VMEM((CH, WIDTH, 2, FC), BF16),
            pltpu.VMEM((CH, WIDTH, 2 * FC), BF16),
            pltpu.VMEM((CH, 6, HALF, 2 * FC), BF16),
            pltpu.VMEM((CH, 2, HALF, 2 * FC), BF16),
            pltpu.VMEM((CH, 2, 2, HALF, 2 * FC), BF16),
            pltpu.VMEM((CH, HALF, 2 * FC), BF16),
            pltpu.VMEM((CH, HALF, 2 * FC), BF16),
            pltpu.VMEM((CH, TOK, 2 * FC), BF16),
            pltpu.VMEM((TOK, WIDTH), F32),
            pltpu.VMEM((2, WIDTH, FC), F32),
            pltpu.VMEM((2, WIDTH, FC), BF16),
            pltpu.VMEM((2, WIDTH, FC), BF16),
            pltpu.VMEM((2, WIDTH, FC), F32),
            pltpu.VMEM((8, OWN, WIDTH), BF16),
            pltpu.VMEM((8, OWN, WIDTH), BF16),
            pltpu.VMEM((7, OWN, WIDTH), BF16),
            dma, dma((3,)), dma, dma((7,)), dma, dma, dma((3, CH)), dma((3, CH)),
            dma((CH, 14)), dma((CH, 14)), dma((2,)), dma((2,)),
        ],
        compiler_params=pltpu.CompilerParams(
            collective_id=0, has_side_effects=True, vmem_limit_bytes=63 * 2**20
        ),
        cost_estimate=pl.CostEstimate(flops=2 * macs, bytes_accessed=40 * 2**20, transcendentals=0),
    )(
        acts.T,
        jnp.transpose(old_weights, (1, 0, 2)),
        jnp.transpose(old_mean, (1, 0, 2)),
        jnp.transpose(old_var, (1, 0, 2)).astype(BF16),
        cotangent,
    )
    return hidden, input_grad.T, new_weights, new_mean, new_var


def solution(mesh):
    placed = (
        P("dp", "mp"),
        P(None, ("mp", "dp"), None),
        P(None, ("mp", "dp"), None),
        P(None, ("mp", "dp"), None),
        P("mp", "dp"),
    )
    return jax.shard_map(
        shards,
        mesh=mesh,
        in_specs=placed,
        out_specs=(
            P("mp", "dp"),
            P("dp", "mp"),
            P(None, "mp", "dp"),
            P(None, "mp", "dp"),
            P(None, "mp", "dp"),
        ),
        check_vma=False,
    )
```

time: 1040 us -> 246 us (0.24)
  waiting for transfers between devices: 526 us -> 0 us
  local copies, waits for them, and re-layouts: 312 us -> 11.2 us
  Pallas kernels: 0 us -> 228 us
  other arithmetic: 84.2 us -> 5.83 us
  blocking collectives: 43.4 us -> 0 us
  matrix products: 43.1 us -> 0 us
  starting transfers between devices: 14.6 us -> 0 us
  between operations: 13.8 us -> 0.65 us
    reduce_scatter x2 -> x0, waiting for transfers between devices: 364 us -> none  [the longest x1 364 us: shards(): lax.psum_scatter(jnp.einsum('td,kdf->tkf', token_cols, weights, preferred...]
    pallas_call x0 -> x1, Pallas kernels: none -> 228 us  [shards(): pl.pallas_call(kernel, out_shape=(jax.ShapeDtypeStruct((HALF, FS), BF16),...]
    unnamed x17 -> x11, local copies, waits for them, and re-layouts: 239 us -> 11.2 us
    all_gather x2 -> x0, waiting for transfers between devices: 161 us -> none  [the longest x1 161 us: shards(): all_grads = lax.all_gather(local_grads, 'mp', axis=0, tiled=True)]
    all_to_all x1 -> x0, other arithmetic: 52.2 us -> none  [relay_variance(): lax.all_to_all(old_var, 'dp', split_axis=2, concat_axis=1, tiled=True)]
    mul x2 -> x0, local copies, waits for them, and re-layouts: 51 us -> none  [the longest x1 25.6 us: adam_update(): beta_two * variance + (1.0 - beta_two) * weight_grads * weight_grads]
    all_to_all x1 -> x0, blocking collectives: 43.4 us -> none  [shards(): lax.all_to_all(old_weights, 'dp', split_axis=2, concat_axis=1, tiled=True)]
    dot_general x3 -> x0, matrix products: 43.1 us -> none  [the longest x1 18.2 us: shards(): jnp.einsum('td,tkf->kdf', token_cols, all_grads, preferred_element_type=j...]
  transfers between devices with their start and end apart: 6 -> 0, of which waited for: 2 -> 0; matrix products, arithmetic and copies ran while one was open for 40% -> 0% of each run, Pallas kernels for 0% -> 0%
where the time goes in v1:
time: 246 us
  Pallas kernels  228 us (93%)
  local copies, waits for them, and re-layouts  11.2 us (5%)
  other arithmetic  5.83 us (2%)
    pallas_call x1, Pallas kernels, shards(): pl.pallas_call(kernel, out_shape=(jax.ShapeDtypeStruct((HALF, FS), BF16),...  228 us
    unnamed x11, local copies, waits for them, and re-layouts  11.2 us
    convert_element_type x1, other arithmetic, shards(): jnp.transpose(old_var, (1, 0, 2)).astype(BF16)  5.83 us

profile of v1, /device:TPU:1, one launch (start us, length us, event | category | flops | bytes accessed | tf_op | source)
XLA Modules:
  0.0 245.6 jit_solution(10185280281943662893)
XLA Ops:
  0.6 5.8 %convert_bitcast_fusion.v_in = bf16[36,2,18432]{2,1,0:T(2,128)(2,1)} fusion(f32[2,36,18432]{2,0,1:T(2,128)} %param.8), kind=kLoop, calls=%fused_computation | loop fusion | flops 1327104 | bytes 7962624 | tf_op jit(solution)/shard_map/convert_element_type | solution.py:440
  6.5 227.8 %shard_map.92 = (bf16[256,1152]{1,0:T(8,128)(2,1)}, bf16[576,128]{1,0:T(8,128)(2,1)}, bf16[2,576,1152]{2,1,0:T(8,128)(2,1)}, bf16[2,576,1152]{2,1,0:T(8,128)(2,1)}, f32[2,576,1152]{2,1,0:T(8,128)}) custom-call(bf16[576,128]{1,0:T(8,128)(2,1)} %bitcast.11, bf16[36,2,18432]{2,1,0:T(2,128)(2,1)} %bitcast.9, bf16[36,2,18432]{2,1,0:T(2,128)(2,1)} %bitcast.10, ...), custom_call_target="tpu_custom_call" | custom-call | flops 16307453952 | bytes 41943040 | tf_op jit(solution)/shard_map/pallas_call | solution.py:397
  234.3 0.0 copy-start
  234.3 2.1 copy.15
  236.4 0.0 slice-start
  236.4 1.7 copy.16
  238.1 0.0 slice-start.1
  238.1 3.5 %copy.17 = bf16[2,576,1152]{2,1,0:T(8,128)(2,1)} copy(bf16[2,576,1152]{2,1,0:T(8,128)(2,1)} %get-tuple-element.22) | data formatting | bytes 5308416
  241.7 0.0 copy-done
  241.7 1.5 copy.18
  243.2 0.0 slice-done
  243.2 0.0 slice-done.1
  243.2 2.4 copy.19
  (1 shorter events, 0.0 us)
Async XLA Ops:
  234.3 7.4 %copy-start = (bf16[2,576,1152]{2,1,0:T(8,128)(2,1)S(1)}, bf16[2,576,1152]{2,1,0:T(8,128)(2,1)}, u32[]{:S(2)}) copy-start(bf16[2,576,1152]{2,1,0:T(8,128)(2,1)} %get-tuple-element.23) | copy-start | bytes 7962628
  236.4 6.8 %slice-start = ((s8[5308416]{0:T(1024)(128)(4,1)}), s8[4194304]{0:T(1024)(128)(4,1)S(1)}, s32[]{:S(2)}) async-start(s8[5308416]{0:T(1024)(128)(4,1)} %bitcast.6), calls=%async_computation | async-start | bytes 8388608
  238.1 5.1 %slice-start.1 = ((s8[5308416]{0:T(1024)(128)(4,1)}), s8[1114112]{0:T(1024)(128)(4,1)S(1)}, s32[]{:S(2)}) async-start(s8[5308416]{0:T(1024)(128)(4,1)} %bitcast.6), calls=%async_computation.1 | async-start | bytes 2228224

commit v2 on v1

--- a/solution.py
+++ b/solution.py
@@ -30,8 +30,10 @@
 BLOCK = TOK // Z
 HALF = BLOCK // LO
 FS = 1152
-CH = 3
+CH = 9
 FC = FS // CH
+LAG = 4
+PIECE = 9
 OWN = TOK // DP
 
 
@@ -50,9 +52,9 @@
 
 def kernel(
     at_in, w_in, m_in, v_in, cot, hid, ig, nw, nm, nv,
-    at, a, wr, mr, vr, wd, sb, rmid, rfin, yls, ylr, grads, acc, gw, nws, nms, nvs, xs, xr, xf,
-    copy_sem, out_sem, act_send, act_recv, fwd_send, fwd_recv, rel_send, rel_recv,
-    zs_sem, zr_sem, x_send, x_recv,
+    vf, vb, at, a, wr, mr, vr, wd, sb, rmid, rfin, yls, ylr, grads, acc, gw, nws, nms, nvs, xs, xr, xq, xf,
+    copy_sem, cast_sem, out_sem, act_send, act_recv, fwd_send, fwd_recv, rel_send, rel_recv,
+    zs_sem, zr_sem, x_send, x_recv, p_send, p_recv,
 ):
     dp, mp = lax.axis_index("dp"), lax.axis_index("mp")
     core = lax.rem(dp, 2)
@@ -83,6 +85,12 @@
         step = q + lax.div(q, 2) * (1 - 2 * lax.rem(q, 2))
         return lax.rem(y_hi + far, 2) * 4 + lax.rem(x + step, 4)
 
+    def cast_part(i):
+        return pltpu.make_async_copy(v_in.at[pl.ds(i * PIECE, PIECE)], vf.at[i % 2], cast_sem.at[i % 2])
+
+    cast_part(0).start()
+    cast_part(1).start()
+
     barrier = pltpu.get_barrier_semaphore()
 
     @pl.loop(0, DP - 1)
@@ -130,10 +138,24 @@
         sent = dst.at[c, pl.ds(0, WIDTH - ROWS)]
         pltpu.make_async_copy(sent, sent, rel_send.at[index, c]).wait()
 
-    for c in range(CH):
+    for c in range(2):
         relay(0, w_in, wr, c)
 
+    for i in range(ROWS // PIECE):
+        cast_part(i).wait()
+
+        @pl.loop(0, PIECE)
+        def _(row):
+            vb[i * PIECE + row] = vf[i % 2, row].astype(BF16)
+
+        if i + 2 < ROWS // PIECE:
+            cast_part(i + 2).start()
+
+    def turn(index):
+        a[pl.ds(pl.multiple_of(index * OWN, OWN), OWN), :] = at[:, cols(index)].T
+
     own_act.wait()
+    turn(dp)
 
     @pl.loop(1, 8)
     def _(i):
@@ -144,13 +166,14 @@
         block = at.at[:, cols(source)]
         remote(block, block, act_send, act_recv.at[i - 1], twin).wait_recv()
         remote(block, block, fwd_send, fwd_recv, twin).start()
+        turn(source)
 
     half_acts = at.at[:, pl.ds(0, TOK // 2)]
     pltpu.make_async_copy(half_acts, half_acts, fwd_recv).wait()
 
-    @pl.loop(0, DP)
+    @pl.loop(0, DP // 2)
     def _(i):
-        a[pl.ds(pl.multiple_of(i * OWN, OWN), OWN), :] = at[:, cols(i)].T
+        turn(i * 2 + 1 - core)
 
     def tokens(step, half):
         return pl.ds(pl.multiple_of(lax.rem(z + step, Z) * BLOCK + half * HALF, HALF), HALF)
@@ -229,10 +252,11 @@
         grads[c, rows, FC : 2 * FC] = (upstream * activated).astype(BF16)
         mine = grads.at[c, rows]
         zsend(c, 7, mine, mine, mate)
+
+    def fifth(c):
+        mine = grads.at[c, tokens(0, lo)]
         zsend(c, 8, mine, mine, plus)
         zsend(c, 9, mine, mine, minus)
-
-    def fifth(c):
         theirs = grads.at[c, tokens(0, 1 - lo)]
         zwait(c, 7, theirs)
         zsend(c, 10, theirs, theirs, plus)
@@ -272,12 +296,12 @@
         ]
 
     def weight_grads(c):
-        @pl.loop(0, 6)
+        @pl.loop(0, 3)
         def _(i):
-            k = lax.rem(i, 2)
-            rows = pl.ds(pl.multiple_of(lax.div(i, 2) * 192, 192), 192)
-            span = pl.ds(pl.multiple_of(k * FC, FC), FC)
-            gw[k, rows, :] = dot(at[rows, :], grads[c, :, span]) * width_scale
+            rows = pl.ds(pl.multiple_of(i * 192, 192), 192)
+            both = dot(at[rows, :], grads[c]) * width_scale
+            gw[0, rows, :] = both[:, :FC]
+            gw[1, rows, :] = both[:, FC:]
 
     def update(c):
         relayed(1, mr, c)
@@ -295,11 +319,11 @@
                 grad = gw[k, rows, :]
                 moment_one = beta_one * mean[k].astype(F32) + (1.0 - beta_one) * grad
                 var_next = beta_two * var[k].astype(F32) + (1.0 - beta_two) * grad * grad
-                mean_hat = moment_one / (1.0 - beta_one**RESUME_STEP)
-                var_hat = var_next / (1.0 - beta_two**RESUME_STEP)
+                mean_hat = moment_one * (1.0 / (1.0 - beta_one**RESUME_STEP))
+                var_hat = var_next * (1.0 / (1.0 - beta_two**RESUME_STEP))
                 master = wd[c, rows, k * FC : (k + 1) * FC].astype(F32)
-                updated = master - learn_rate * (
-                    mean_hat / (jnp.sqrt(var_hat) + epsilon) + decay_rate * master
+                updated = master * (1.0 - learn_rate * decay_rate) - learn_rate * mean_hat / (
+                    jnp.sqrt(var_hat) + epsilon
                 )
                 nws[k, rows, :] = updated.astype(BF16)
                 nms[k, rows, :] = moment_one.astype(BF16)
@@ -308,73 +332,81 @@
         for copy in written(c):
             copy.start()
 
-    first(0)
-    relay(1, m_in, mr, 0)
-    first(1)
-    second(0)
-    relay(2, v_in, vr, 0)
-    first(2)
-    second(1)
-    relay(1, m_in, mr, 1)
-    third(0)
-    fourth(0)
-    second(2)
-    relay(2, v_in, vr, 1)
-    fifth(0)
-    third(1)
-    fourth(1)
-    relay(1, m_in, mr, 2)
-    sixth(0)
-    fifth(1)
-    third(2)
-    fourth(2)
-    relay(2, v_in, vr, 2)
-    gathered(0)
-    fifth(2)
-    sixth(1)
-    back(0)
-    weight_grads(0)
-    update(0)
-    sixth(2)
-    gathered(1)
-    back(1)
-    weight_grads(1)
-    update(1)
-    gathered(2)
-    back(2)
+    def stages(step):
+        def at_lag(lag):
+            return 0 <= step - lag < CH
+
+        if at_lag(0):
+            first(step)
+        if at_lag(1):
+            second(step - 1)
+        if step + 2 < CH:
+            relay(0, w_in, wr, step + 2)
+        if at_lag(2):
+            third(step - 2)
+        if at_lag(3):
+            fourth(step - 3)
+            relay(1, m_in, mr, step - 3)
+        if at_lag(4):
+            relay(2, vb, vr, step - 4)
+        if at_lag(LAG):
+            fifth(step - LAG)
+        if at_lag(LAG + 1):
+            sixth(step - LAG - 1)
+        if at_lag(LAG + 2) and step - LAG - 2 < CH - 1:
+            gathered(step - LAG - 2)
+            back(step - LAG - 2)
+            weight_grads(step - LAG - 2)
+            update(step - LAG - 2)
+
+    for step in range(CH + LAG + 2):
+        stages(step)
+
+    gathered(CH - 1)
+
+    def swap(j):
+        return remote(xs.at[j], xr.at[j], x_send.at[j], x_recv.at[j], twin)
 
     def acc_rows(index):
         return pl.ds(pl.multiple_of(index * OWN, OWN), OWN)
 
-    @pl.loop(0, 8)
-    def _(j):
+    @pl.loop(1, 9)
+    def _(i):
+        j = peer_line(lax.rem(i, 8))
+        rows = pl.ds(pl.multiple_of(j * HALF, HALF), HALF)
+        acc[rows, :] += lax.dot_general(
+            grads[CH - 1, rows, :], wd[CH - 1], (((1,), (1,)), ((), ())), preferred_element_type=F32
+        )
         xs[j] = acc[acc_rows(j * 2 + 1 - core), :].astype(BF16)
-
-    swap = remote(xs, xr, x_send.at[0], x_recv.at[0], twin)
-    swap.start()
-    weight_grads(2)
-    swap.wait()
-
-    @pl.loop(0, 8)
-    def _(j):
+        swap(j).start()
+
+    @pl.loop(1, 9)
+    def _(i):
+        j = peer_line(lax.rem(i, 8))
+        swap(j).wait_recv()
         rows = acc_rows(j * 2 + core)
         total = acc[rows, :] + xr[j].astype(F32)
         acc[rows, :] = total
-        xs[j] = total.astype(BF16)
-
-    @pl.loop(1, 8)
-    def _(i):
-        owner = peer_line(i)
-        remote(xs.at[owner], xf.at[i - 1], x_send.at[1], x_recv.at[1], (owner * 2 + core, mp)).start()
-
-    update(2)
-    pltpu.make_async_copy(xf, xf, x_recv.at[1]).wait()
+
+        @pl.when(i < 8)
+        def _():
+            xq[i - 1] = total.astype(BF16)
+            remote(xq.at[i - 1], xf.at[i - 1], p_send, p_recv, (j * 2 + core, mp)).start()
+
+    weight_grads(CH - 1)
+    update(CH - 1)
+    pltpu.make_async_copy(xf, xf, p_recv).wait()
     total = acc[acc_rows(dp), :]
     for i in range(7):
         total = total + xf[i].astype(F32)
     ig[...] = (total * width_scale).T.astype(BF16)
 
-    pltpu.make_async_copy(xf, xf, x_send.at[1]).wait()
+    pltpu.make_async_copy(xf, xf, p_send).wait()
+
+    @pl.loop(0, 8)
+    def _(j):
+        swap(j).wait_send()
+
     for copy in written(CH - 1):
         copy.wait()
     for copy in sends:
@@ -406,6 +438,8 @@
         in_specs=[hbm, hbm, hbm, hbm, vmem],
         out_specs=(vmem, vmem, hbm, hbm, hbm),
         scratch_shapes=[
+            pltpu.VMEM((2, PIECE, 2, FS * DP), F32),
+            pltpu.VMEM((ROWS, 2, FS * DP), BF16),
             pltpu.VMEM((WIDTH, TOK), BF16),
             pltpu.VMEM((TOK, WIDTH), BF16),
             pltpu.VMEM((CH, WIDTH, 2, FC), BF16),
@@ -426,8 +460,9 @@
             pltpu.VMEM((8, OWN, WIDTH), BF16),
             pltpu.VMEM((8, OWN, WIDTH), BF16),
             pltpu.VMEM((7, OWN, WIDTH), BF16),
-            dma, dma((3,)), dma, dma((7,)), dma, dma, dma((3, CH)), dma((3, CH)),
-            dma((CH, 14)), dma((CH, 14)), dma((2,)), dma((2,)),
+            pltpu.VMEM((7, OWN, WIDTH), BF16),
+            dma, dma((2,)), dma((3,)), dma, dma((7,)), dma, dma, dma((3, CH)), dma((3, CH)),
+            dma((CH, 14)), dma((CH, 14)), dma((8,)), dma((8,)), dma, dma,
         ],
         compiler_params=pltpu.CompilerParams(
             collective_id=0, has_side_effects=True, vmem_limit_bytes=63 * 2**20
@@ -437,7 +472,7 @@
         acts.T,
         jnp.transpose(old_weights, (1, 0, 2)),
         jnp.transpose(old_mean, (1, 0, 2)),
-        jnp.transpose(old_var, (1, 0, 2)).astype(BF16),
+        jnp.transpose(old_var, (1, 0, 2)),
         cotangent,
     )
     return hidden, input_grad.T, new_weights, new_mean, new_var

time: 246 us -> 229 us (0.931)
  Pallas kernels: 228 us -> 217 us
  other arithmetic: 5.83 us -> 0.01 us
    pallas_call x1, Pallas kernels: 228 us -> 217 us  [shards(): pl.pallas_call(kernel, out_shape=(jax.ShapeDtypeStruct((HALF, FS), BF16),...]
    convert_element_type x1 -> x0, other arithmetic: 5.83 us -> none  [shards(): jnp.transpose(old_var, (1, 0, 2)).astype(BF16)]
where the time goes in v2:
time: 229 us
  Pallas kernels  217 us (95%)
  local copies, waits for them, and re-layouts  11.2 us (5%)
    pallas_call x1, Pallas kernels, shards(): pl.pallas_call(kernel, out_shape=(jax.ShapeDtypeStruct((HALF, FS), BF16),...  217 us
    unnamed x11, local copies, waits for them, and re-layouts  11.2 us

profile of v2, /device:TPU:1, one launch (start us, length us, event | category | flops | bytes accessed | tf_op | source)
XLA Modules:
  0.0 228.5 jit_solution(7318867924905872375)
XLA Ops:
  0.6 216.6 %shard_map.92 = (bf16[256,1152]{1,0:T(8,128)(2,1)}, bf16[576,128]{1,0:T(8,128)(2,1)}, bf16[2,576,1152]{2,1,0:T(8,128)(2,1)}, bf16[2,576,1152]{2,1,0:T(8,128)(2,1)}, f32[2,576,1152]{2,1,0:T(8,128)}) custom-call(bf16[576,128]{1,0:T(8,128)(2,1)} %bitcast.11, bf16[36,2,18432]{2,1,0:T(2,128)(2,1)} %bitcast.9, bf16[36,2,18432]{2,1,0:T(2,128)(2,1)} %bitcast.10, ...), custom_call_target="tpu_custom_call" | custom-call | flops 16307453952 | bytes 41943040 | tf_op jit(solution)/shard_map/pallas_call | solution.py:429
  217.3 0.0 copy-start
  217.3 2.1 copy.15
  219.4 0.0 slice-start
  219.4 1.7 copy.16
  221.1 0.0 slice-start.1
  221.1 3.5 %copy.17 = bf16[2,576,1152]{2,1,0:T(8,128)(2,1)} copy(bf16[2,576,1152]{2,1,0:T(8,128)(2,1)} %get-tuple-element.22) | data formatting | bytes 5308416
  224.6 0.0 copy-done
  224.6 1.5 copy.18
  226.1 0.0 slice-done
  226.2 0.0 slice-done.1
  226.2 2.4 %copy.19 = f32[2,576,1152]{2,1,0:T(8,128)} copy(f32[2,576,1152]{2,1,0:T(8,128)S(1)} %bitcast.6) | data formatting | bytes 10616832
  (1 shorter events, 0.0 us)
Async XLA Ops:
  217.3 7.4 %copy-start = (bf16[2,576,1152]{2,1,0:T(8,128)(2,1)S(1)}, bf16[2,576,1152]{2,1,0:T(8,128)(2,1)}, u32[]{:S(2)}) copy-start(bf16[2,576,1152]{2,1,0:T(8,128)(2,1)} %get-tuple-element.23) | copy-start | bytes 7962628
  219.4 6.8 %slice-start = ((s8[5308416]{0:T(1024)(128)(4,1)}), s8[4194304]{0:T(1024)(128)(4,1)S(1)}, s32[]{:S(2)}) async-start(s8[5308416]{0:T(1024)(128)(4,1)} %bitcast.5), calls=%async_computation | async-start | bytes 8388608
  221.1 5.1 %slice-start.1 = ((s8[5308416]{0:T(1024)(128)(4,1)}), s8[1114112]{0:T(1024)(128)(4,1)S(1)}, s32[]{:S(2)}) async-start(s8[5308416]{0:T(1024)(128)(4,1)} %bitcast.5), calls=%async_computation.1 | async-start | bytes 2228224

commit v3 on v2

--- a/solution.py
+++ b/solution.py
@@ -32,6 +32,8 @@
 FS = 1152
 CH = 9
 FC = FS // CH
+AHEAD = 4
+LATE = 2
 LAG = 4
 PIECE = 9
 OWN = TOK // DP
@@ -116,7 +118,7 @@
     def _(i):
         remote(at_in, at.at[:, cols(dp)], act_send, act_recv.at[i - 1], (peer_line(i) * 2 + core, mp)).start()
 
-    remote(at_in, at.at[:, cols(dp)], fwd_send, fwd_recv, twin).start()
+    remote(at_in, at.at[:, cols(dp)], fwd_send, fwd_recv.at[line], twin).start()
 
     def relay(index, src, dst, c):
         mine = pl.ds(dp * ROWS, ROWS)
@@ -138,7 +140,7 @@
         sent = dst.at[c, pl.ds(0, WIDTH - ROWS)]
         pltpu.make_async_copy(sent, sent, rel_send.at[index, c]).wait()
 
-    for c in range(2):
+    for c in range(AHEAD):
         relay(0, w_in, wr, c)
 
     for i in range(ROWS // PIECE):
@@ -165,15 +167,20 @@
         source = (lax.rem(y_hi + far, 2) * 4 + lax.rem(x + 4 - step, 4)) * 2 + core
         block = at.at[:, cols(source)]
         remote(block, block, act_send, act_recv.at[i - 1], twin).wait_recv()
-        remote(block, block, fwd_send, fwd_recv, twin).start()
+        remote(block, block, fwd_send, fwd_recv.at[lax.div(source, 2)], twin).start()
         turn(source)
 
     half_acts = at.at[:, pl.ds(0, TOK // 2)]
-    pltpu.make_async_copy(half_acts, half_acts, fwd_recv).wait()
 
     @pl.loop(0, DP // 2)
     def _(i):
-        turn(i * 2 + 1 - core)
+        far = lax.rem(i, 2)
+        q = lax.div(i, 2)
+        step = q + lax.div(q, 2) * (1 - 2 * lax.rem(q, 2))
+        origin = lax.rem(y_hi + far, 2) * 4 + lax.rem(x + 4 - step, 4)
+        block = at.at[:, cols(origin * 2 + 1 - core)]
+        remote(block, block, fwd_send, fwd_recv.at[origin], twin).wait_recv()
+        turn(origin * 2 + 1 - core)
 
     def tokens(step, half):
         return pl.ds(pl.multiple_of(lax.rem(z + step, Z) * BLOCK + half * HALF, HALF), HALF)
@@ -198,16 +205,17 @@
             wd[c, rows, 0:FC] = pair[0]
             wd[c, rows, FC : 2 * FC] = pair[1]
 
-        @pl.loop(0, 4)
+        @pl.loop(0, 2)
         def _(slot):
-            late = lax.div(slot, 2)
-            odd = lax.rem(slot, 2)
-            step = 2 + late * (2 * odd - 1)
-            half = odd + late * (1 - 2 * odd)
-            sb[c, slot] = dot(a[tokens(step, half), :], wd[c]).astype(BF16)
+            sb[c, slot] = dot(a[tokens(2, slot), :], wd[c]).astype(BF16)
 
         zsend(c, 0, sb.at[c, 0], rmid.at[c, 0], plus)
         zsend(c, 1, sb.at[c, 1], rmid.at[c, 1], minus)
+
+        @pl.loop(0, 2)
+        def _(slot):
+            sb[c, 2 + slot] = dot(a[tokens(1 + 2 * slot, 1 - slot), :], wd[c]).astype(BF16)
+
         zsend(c, 2, sb.at[c, 2], rfin.at[c, 0, 1], plus)
         zsend(c, 3, sb.at[c, 3], rfin.at[c, 1, 0], minus)
 
@@ -340,8 +348,8 @@
             first(step)
         if at_lag(1):
             second(step - 1)
-        if step + 2 < CH:
-            relay(0, w_in, wr, step + 2)
+        if step + AHEAD < CH:
+            relay(0, w_in, wr, step + AHEAD)
         if at_lag(2):
             third(step - 2)
         if at_lag(3):
@@ -356,8 +364,9 @@
         if at_lag(LAG + 2) and step - LAG - 2 < CH - 1:
             gathered(step - LAG - 2)
             back(step - LAG - 2)
-            weight_grads(step - LAG - 2)
-            update(step - LAG - 2)
+            if step - LAG - 2 < CH - LATE:
+                weight_grads(step - LAG - 2)
+                update(step - LAG - 2)
 
     for step in range(CH + LAG + 2):
         stages(step)
@@ -393,8 +402,10 @@
             xq[i - 1] = total.astype(BF16)
             remote(xq.at[i - 1], xf.at[i - 1], p_send, p_recv, (j * 2 + core, mp)).start()
 
-    weight_grads(CH - 1)
-    update(CH - 1)
+    for c in range(CH - LATE, CH):
+        weight_grads(c)
+        update(c)
+
     pltpu.make_async_copy(xf, xf, p_recv).wait()
     total = acc[acc_rows(dp), :]
     for i in range(7):
@@ -461,7 +472,7 @@
             pltpu.VMEM((8, OWN, WIDTH), BF16),
             pltpu.VMEM((7, OWN, WIDTH), BF16),
             pltpu.VMEM((7, OWN, WIDTH), BF16),
-            dma, dma((2,)), dma((3,)), dma, dma((7,)), dma, dma, dma((3, CH)), dma((3, CH)),
+            dma, dma((2,)), dma((3,)), dma, dma((7,)), dma, dma((DP // 2,)), dma((3, CH)), dma((3, CH)),
             dma((CH, 14)), dma((CH, 14)), dma((8,)), dma((8,)), dma, dma,
         ],
         compiler_params=pltpu.CompilerParams(

time: 229 us -> 225 us (0.983)
  Pallas kernels: 217 us -> 212 us
    pallas_call x1, Pallas kernels: 217 us -> 212 us  [shards(): pl.pallas_call(kernel, out_shape=(jax.ShapeDtypeStruct((HALF, FS), BF16),...]
where the time goes in v3:
time: 225 us; the launch traced here: 224 us
  Pallas kernels  212 us (94%)
  local copies, waits for them, and re-layouts  11.2 us (5%)
    pallas_call x1, Pallas kernels, shards(): pl.pallas_call(kernel, out_shape=(jax.ShapeDtypeStruct((HALF, FS), BF16),...  212 us
    unnamed x11, local copies, waits for them, and re-layouts  11.2 us

profile of v3, /device:TPU:1, one launch (start us, length us, event | category | flops | bytes accessed | tf_op | source)
XLA Modules:
  0.0 224.0 jit_solution(9351276175558361423)
XLA Ops:
  0.6 212.1 %shard_map.92 = (bf16[256,1152]{1,0:T(8,128)(2,1)}, bf16[576,128]{1,0:T(8,128)(2,1)}, bf16[2,576,1152]{2,1,0:T(8,128)(2,1)}, bf16[2,576,1152]{2,1,0:T(8,128)(2,1)}, f32[2,576,1152]{2,1,0:T(8,128)}) custom-call(bf16[576,128]{1,0:T(8,128)(2,1)} %bitcast.11, bf16[36,2,18432]{2,1,0:T(2,128)(2,1)} %bitcast.9, bf16[36,2,18432]{2,1,0:T(2,128)(2,1)} %bitcast.10, ...), custom_call_target="tpu_custom_call" | custom-call | flops 16307453952 | bytes 41943040 | tf_op jit(solution)/shard_map/pallas_call | solution.py:440
  212.8 0.0 copy-start
  212.8 2.1 copy.15
  214.9 0.0 slice-start
  214.9 1.7 copy.16
  216.6 0.0 slice-start.1
  216.6 3.5 %copy.17 = bf16[2,576,1152]{2,1,0:T(8,128)(2,1)} copy(bf16[2,576,1152]{2,1,0:T(8,128)(2,1)} %get-tuple-element.22) | data formatting | bytes 5308416
  220.2 0.0 copy-done
  220.2 1.5 copy.18
  221.7 0.0 slice-done
  221.7 0.0 slice-done.1
  221.7 2.4 %copy.19 = f32[2,576,1152]{2,1,0:T(8,128)} copy(f32[2,576,1152]{2,1,0:T(8,128)S(1)} %bitcast.6) | data formatting | bytes 10616832
  (1 shorter events, 0.0 us)
Async XLA Ops:
  212.8 7.4 %copy-start = (bf16[2,576,1152]{2,1,0:T(8,128)(2,1)S(1)}, bf16[2,576,1152]{2,1,0:T(8,128)(2,1)}, u32[]{:S(2)}) copy-start(bf16[2,576,1152]{2,1,0:T(8,128)(2,1)} %get-tuple-element.23) | copy-start | bytes 7962628
  214.9 6.8 %slice-start = ((s8[5308416]{0:T(1024)(128)(4,1)}), s8[4194304]{0:T(1024)(128)(4,1)S(1)}, s32[]{:S(2)}) async-start(s8[5308416]{0:T(1024)(128)(4,1)} %bitcast.5), calls=%async_computation | async-start | bytes 8388608
  216.6 5.1 %slice-start.1 = ((s8[5308416]{0:T(1024)(128)(4,1)}), s8[1114112]{0:T(1024)(128)(4,1)S(1)}, s32[]{:S(2)}) async-start(s8[5308416]{0:T(1024)(128)(4,1)} %bitcast.5), calls=%async_computation.1 | async-start | bytes 2228224

commit v4 on v3

--- a/solution.py
+++ b/solution.py
@@ -54,7 +54,7 @@
 
 def kernel(
     at_in, w_in, m_in, v_in, cot, hid, ig, nw, nm, nv,
-    vf, vb, at, a, wr, mr, vr, wd, sb, rmid, rfin, yls, ylr, grads, acc, gw, nws, nms, nvs, xs, xr, xq, xf,
+    vf, vb, at, a, wr, mr, vr, wd, sb, rmid, rfin, yls, ylr, grads, acc, gw, nws, nms, nvs, xr, xq, xf,
     copy_sem, cast_sem, out_sem, act_send, act_recv, fwd_send, fwd_recv, rel_send, rel_recv,
     zs_sem, zr_sem, x_send, x_recv, p_send, p_recv,
 ):
@@ -373,11 +373,11 @@
 
     gathered(CH - 1)
 
-    def swap(j):
-        return remote(xs.at[j], xr.at[j], x_send.at[j], x_recv.at[j], twin)
-
     def acc_rows(index):
         return pl.ds(pl.multiple_of(index * OWN, OWN), OWN)
+
+    def swap(j):
+        return remote(acc.at[acc_rows(j * 2 + 1 - core)], xr.at[j], x_send.at[j], x_recv.at[j], twin)
 
     @pl.loop(1, 9)
     def _(i):
@@ -386,7 +386,6 @@
         acc[rows, :] += lax.dot_general(
             grads[CH - 1, rows, :], wd[CH - 1], (((1,), (1,)), ((), ())), preferred_element_type=F32
         )
-        xs[j] = acc[acc_rows(j * 2 + 1 - core), :].astype(BF16)
         swap(j).start()
 
     @pl.loop(1, 9)
@@ -394,7 +393,7 @@
         j = peer_line(lax.rem(i, 8))
         swap(j).wait_recv()
         rows = acc_rows(j * 2 + core)
-        total = acc[rows, :] + xr[j].astype(F32)
+        total = acc[rows, :] + xr[j]
         acc[rows, :] = total
 
         @pl.when(i < 8)
@@ -468,8 +467,7 @@
             pltpu.VMEM((2, WIDTH, FC), BF16),
             pltpu.VMEM((2, WIDTH, FC), BF16),
             pltpu.VMEM((2, WIDTH, FC), F32),
-            pltpu.VMEM((8, OWN, WIDTH), BF16),
-            pltpu.VMEM((8, OWN, WIDTH), BF16),
+            pltpu.VMEM((8, OWN, WIDTH), F32),
             pltpu.VMEM((7, OWN, WIDTH), BF16),
             pltpu.VMEM((7, OWN, WIDTH), BF16),
             dma, dma((2,)), dma((3,)), dma, dma((7,)), dma, dma((DP // 2,)), dma((3, CH)), dma((3, CH)),

time: 225 us -> 226 us (level)
  no operation moved by 1% of the time
where the time goes in v4:
time: 226 us
  Pallas kernels  214 us (95%)
  local copies, waits for them, and re-layouts  11.2 us (5%)
    pallas_call x1, Pallas kernels, shards(): pl.pallas_call(kernel, out_shape=(jax.ShapeDtypeStruct((HALF, FS), BF16),...  214 us
    unnamed x11, local copies, waits for them, and re-layouts  11.2 us

profile of v4, /device:TPU:1, one launch (start us, length us, event | category | flops | bytes accessed | tf_op | source)
XLA Modules:
  0.0 226.1 jit_solution(2958245685063522110)
XLA Ops:
  0.6 214.2 %shard_map.92 = (bf16[256,1152]{1,0:T(8,128)(2,1)}, bf16[576,128]{1,0:T(8,128)(2,1)}, bf16[2,576,1152]{2,1,0:T(8,128)(2,1)}, bf16[2,576,1152]{2,1,0:T(8,128)(2,1)}, f32[2,576,1152]{2,1,0:T(8,128)}) custom-call(bf16[576,128]{1,0:T(8,128)(2,1)} %bitcast.11, bf16[36,2,18432]{2,1,0:T(2,128)(2,1)} %bitcast.9, bf16[36,2,18432]{2,1,0:T(2,128)(2,1)} %bitcast.10, ...), custom_call_target="tpu_custom_call" | custom-call | flops 16307453952 | bytes 41943040 | tf_op jit(solution)/shard_map/pallas_call | solution.py:439
  214.9 0.0 copy-start
  214.9 2.1 copy.15
  217.0 0.0 slice-start
  217.0 1.7 copy.16
  218.7 0.0 slice-start.1
  218.7 3.5 %copy.17 = bf16[2,576,1152]{2,1,0:T(8,128)(2,1)} copy(bf16[2,576,1152]{2,1,0:T(8,128)(2,1)} %get-tuple-element.22) | data formatting | bytes 5308416
  222.2 0.0 copy-done
  222.2 1.5 copy.18
  223.8 0.0 slice-done
  223.8 0.0 slice-done.1
  223.8 2.4 %copy.19 = f32[2,576,1152]{2,1,0:T(8,128)} copy(f32[2,576,1152]{2,1,0:T(8,128)S(1)} %bitcast.6) | data formatting | bytes 10616832
  (1 shorter events, 0.0 us)
Async XLA Ops:
  214.9 7.4 %copy-start = (bf16[2,576,1152]{2,1,0:T(8,128)(2,1)S(1)}, bf16[2,576,1152]{2,1,0:T(8,128)(2,1)}, u32[]{:S(2)}) copy-start(bf16[2,576,1152]{2,1,0:T(8,128)(2,1)} %get-tuple-element.23) | copy-start | bytes 7962628
  217.0 6.8 %slice-start = ((s8[5308416]{0:T(1024)(128)(4,1)}), s8[4194304]{0:T(1024)(128)(4,1)S(1)}, s32[]{:S(2)}) async-start(s8[5308416]{0:T(1024)(128)(4,1)} %bitcast.5), calls=%async_computation | async-start | bytes 8388608
  218.7 5.1 %slice-start.1 = ((s8[5308416]{0:T(1024)(128)(4,1)}), s8[1114112]{0:T(1024)(128)(4,1)S(1)}, s32[]{:S(2)}) async-start(s8[5308416]{0:T(1024)(128)(4,1)} %bitcast.5), calls=%async_computation.1 | async-start | bytes 2228224
